TPU v7x, 256 devices: a whole 4x4x8 slice. The times are simulated.
256 devices in a mesh: freq: 2 (over core), xs: 64 (over z, y, x_hi), yh: 2 (over x_lo).
Axes of the slice: x: 4 (x_hi: 2, x_lo: 2; x = x_hi * 2 + x_lo), y: 4, z: 8, core: 2. Of those that a mesh axis runs over, the one named last changes fastest.
Arguments:
- field: float32 [2, 64, 1024, 2048], P(None, 'freq', 'xs', 'yh'), may hold values from -6 to 6
- spectral_phase: float32 [64, 2048], P('freq'), may hold values from -3.140625 to 3.140625
- chirp_shift: int32 [64], P('freq'), may hold values from -4 to 4, as said below
- tile_map: int32 [256], P('xs'), may hold values from 0 to 3
- tile_phase: float32 [4, 64], P(None, 'freq'), may hold values from -3.140625 to 3.140625
Outputs:
- pulse: float32 [2, 32, 1024, 2048], P(None, None, 'xs', ('freq', 'yh'))
Inputs may be any that keep to these rules, and one draw needn't show every extreme that they name: `chirp_shift`: some frequency has the offset 4 and another the offset -4.
All inputs are finite; a program needn't handle non-finite values.
Results may differ from a plain program's by a relative error of at most 0.0003.
Values sent between devices are 32-bit elements; how exact they have to be, the bound alone decides.
A program may use at most 128 MiB of HBM per device.

v0:
```python
import functools
import math

import jax
import jax.numpy as jnp
import numpy as np
from jax import lax
from jax.experimental import pallas as pl
from jax.experimental.pallas import tpu as pltpu
from jax.sharding import PartitionSpec as P

NF = 64
NY = 2048
NT = 32
BF = jnp.bfloat16
F32 = jnp.float32
AXES = ("freq", "xs", "yh")
MESH = pl.DeviceIdType.MESH


def dft_tables():
    m = np.arange(256)
    angle = 2.0 * np.pi * (np.outer(m, m) % 256) / 256
    waves = np.stack([np.cos(angle), np.sin(angle)]) / math.sqrt(NY)
    odd_order = np.concatenate([np.arange(64) + 64 * b for b in (1, 0, 3, 2)])
    turn = 2.0 * np.pi * np.outer(np.arange(8), m) / NY
    twiddle = np.stack([np.cos(turn), np.sin(turn)])
    return np.stack([waves, waves[:, :, odd_order]]).astype(np.float32), twiddle.astype(np.float32)


def split(value):
    high = value.astype(BF)
    return high, (value - high.astype(F32)).astype(BF)


def dot(a, b):
    return jnp.dot(a, b, preferred_element_type=F32)


def dot_t(a, b):
    return lax.dot_general(a, b, (((1,), (1,)), ((), ())), preferred_element_type=F32)


def butterflies(re, im, tw):
    a = [(re[:, 256 * c : 256 * c + 256], im[:, 256 * c : 256 * c + 256]) for c in range(4)]
    r = math.sqrt(0.5)

    def add(u, v):
        return u[0] + v[0], u[1] + v[1]

    def sub(u, v):
        return u[0] - v[0], u[1] - v[1]

    def mi(u):
        return u[1], -u[0]

    def four(b):
        e0, e1 = add(b[0], b[2]), sub(b[0], b[2])
        e2, e3 = add(b[1], b[3]), mi(sub(b[1], b[3]))
        return add(e0, e2), add(e1, e3), sub(e0, e2), sub(e1, e3)

    even = four(a)
    b1 = ((a[1][0] + a[1][1]) * r, (a[1][1] - a[1][0]) * r)
    b3 = ((a[3][1] - a[3][0]) * r, (-a[3][0] - a[3][1]) * r)
    odd = four((a[0], b1, mi(a[2]), b3))
    both = []
    for side, parts in enumerate((even, odd)):
        row = []
        for j in range(4):
            p = 2 * j + side
            u = parts[j]
            if p:
                c, s = tw[0, p : p + 1, :], tw[1, p : p + 1, :]
                u = u[0] * c + u[1] * s, u[1] * c - u[0] * s
            row.append(u)
        both.append(row)
    return both


def kernel(
    strips, field, phi_hbm, waves_hbm, tw_hbm, shift_row, tile_phase, tile_ids, out,
    flat, snd, keep, other, halo_a, halo_b, prm, prm_out, prm_in, prm_pair,
    phi, waves, tw, e_own, e_other, t_hi, t_lo, perm, ww, w_lo, wh, wh_lo,
    l_hi, l_lo, spec, near, near_in, side, side_in, pp, opp, relay_in, cross, cross_in, *rest,
):
    by_lane = rest[:4]
    (load_sem, snd_s, snd_r, ha_s, ha_r, hb_s, hb_r, prm_s, prm_r,
     near_s, near_r, row_s, row_r, all_s, all_r, rel_s, rel_r, crs_s, crs_r) = rest[4:]
    g, s, h = (lax.axis_index(a) for a in AXES)
    odd = lax.rem(s, 2)
    pair = s + 1 - 2 * odd
    onward = lax.rem(s + strips + 4 * odd - 2, strips)
    back = lax.rem(s + strips + 2 - 4 * odd, strips)
    core = (1 - g, s, h)

    def peer(dg, ds, dh):
        return (lax.rem(g + dg, 2), pair if ds else s, lax.rem(h + dh, 2))

    def remote(src, dst, a, b, to):
        return pltpu.make_async_remote_copy(
            src_ref=src, dst_ref=dst, send_sem=a, recv_sem=b, device_id=to, device_id_type=MESH
        )

    def block_of(n):
        return n + odd * (3 - 2 * n)

    loads = [
        pltpu.make_async_copy(field.at[:, :, pl.ds(128 * y, 128)], flat.at[y], load_sem.at[y]) for y in range(8)
    ]
    tables = [
        pltpu.make_async_copy(src, dst, load_sem.at[8 + k])
        for k, (src, dst) in enumerate(((waves_hbm, waves), (tw_hbm, tw), (phi_hbm, phi)))
    ]
    for c in loads + tables:
        c.start()
    barrier = pltpu.get_barrier_semaphore()
    greet = [core, peer(0, 0, 1), peer(1, 0, 1), peer(0, 1, 1), peer(1, 1, 1), (g, onward, h), (g, back, h)]
    for to in greet:
        pl.semaphore_signal(barrier, inc=1, device_id=to, device_id_type=MESH)

    def snd_copy(i):
        return remote(snd.at[i], other.at[i], snd_s.at[i], snd_r.at[i], core)

    def a_copy(i):
        return remote(keep.at[i], halo_a.at[i], ha_s.at[i], ha_r.at[i], (g, onward, h))

    def b_copy(i):
        return remote(other.at[i], halo_b.at[i], hb_s.at[i], hb_r.at[i], (g, onward, h))

    def gather_rows(i, whose, into):
        row = 4 * block_of(lax.rem(i, 4)) + 2 * whose + i // 4
        for c in range(2):
            for y in range(8):
                into[i, c, :, 128 * y : 128 * y + 128] = flat[y, c, pl.ds(row, 32, stride=16), :]

    gap = jnp.zeros((8, 32), F32)
    rows = jnp.concatenate([shift_row[...].astype(F32), tile_phase[...], jnp.zeros((3, 32), F32)], axis=0)
    prm[0:8, :] = jnp.concatenate([rows, gap, rows, gap], axis=1)
    for rb in range(4):
        prm[8 + rb : 9 + rb, :] = jnp.full((1, 128), tile_ids[rb], jnp.int32).astype(F32)
    prm[12:16, :] = jnp.zeros((4, 128), F32)
    prm_out[...] = pltpu.roll(prm[...], 32, 1)
    prm_core = remote(prm_out, prm_in, prm_s.at[0], prm_r.at[0], core)
    prm_strip = remote(prm, prm_pair, prm_s.at[1], prm_r.at[1], peer(0, 1, 1))

    for c in loads:
        c.wait()

    def pack_first(i, carry):
        gather_rows(i, g, keep)
        return carry

    def pack_send(i, carry):
        gather_rows(i, 1 - g, snd)
        snd_copy(i).start()
        return carry

    def pack_keep(i, carry):
        gather_rows(i, g, keep)
        return carry

    lax.fori_loop(0, 2, pack_first, 0)
    pl.semaphore_wait(barrier, len(greet))
    a_copy(0).start()
    a_copy(1).start()
    lax.fori_loop(0, 8, pack_send, 0)
    prm_core.start()
    prm_strip.start()
    lax.fori_loop(2, 8, pack_keep, 0)
    for i in range(2):
        snd_copy(i).wait_recv()
        b_copy(i).start()

    for c in tables:
        c.wait()
    lane = lax.broadcasted_iota(jnp.int32, (512, 512), 0)
    wave = lax.broadcasted_iota(jnp.int32, (512, 512), 1)
    turn = lax.rem(lane, 128)
    for half in range(2):
        late = (turn >= 64).astype(jnp.int32)
        late = late if half == 0 else 1 - late
        perm[half] = (8 * lax.rem(turn, 64) + 2 * (lane // 128) + late == wave).astype(F32).astype(BF)
        c_hi, c_lo = split(waves[half, 0])
        s_hi, s_lo = split(waves[half, 1])
        for table, c, w in ((t_hi, c_hi, s_hi), (t_lo, c_lo, s_lo)):
            table[half, 0:256, 0:256] = c
            table[half, 0:256, 256:512] = -w
            table[half, 256:512, 0:256] = w
            table[half, 256:512, 256:512] = c

    lanes = lax.rem(lax.broadcasted_iota(jnp.int32, (1, 512), 1), 128)
    for b in range(4):
        x = phi[:, 512 * b : 512 * b + 512]
        late = lanes >= 64 if b % 2 == 0 else lanes < 64
        sign = 1.0 - 2.0 * jnp.where(late, h, 0).astype(F32)
        for part, value in enumerate((jnp.cos(x), jnp.sin(x))):
            hi, lo = split(value)
            e_own[part, :, 512 * b : 512 * b + 512] = (dot_t(hi, perm[b % 2]) + dot_t(lo, perm[b % 2])) * sign
    e_copy = remote(e_own, e_other, prm_s.at[2], prm_r.at[2], core)
    e_copy.start()

    prm_core.wait()
    prm_strip.wait()
    both = prm[...] + prm_in[...]
    shift = both[0:1, :]
    col = lax.broadcasted_iota(jnp.int32, (NT, 128), 1)
    freq = lax.rem(lax.rem(col, 64) + 32 * g, NF)
    angle = (2.0 * math.pi / NF) * lax.rem(lax.broadcasted_iota(jnp.int32, (NT, 128), 0) * freq, NF).astype(F32)
    scale = 1.0 / math.sqrt(NF)
    real_in = col < 64

    def base(tile):
        phase = jnp.zeros((1, 128), F32)
        for t in range(4):
            phase = phase + jnp.where(tile == float(t), both[1 + t : 2 + t, :], 0.0)
        re, im = jnp.cos(angle + phase) * scale, jnp.sin(angle + phase) * scale
        return jnp.concatenate([jnp.where(real_in, re, -im), jnp.where(real_in, im, re)], axis=0)

    far = (4 * (1 - 2 * odd)).astype(F32)
    inside = jnp.where(odd == 1, (s > 1).astype(F32), (s < strips - 2).astype(F32))
    for nd in range(4):
        dest = block_of(nd)
        here, there = base(prm[8 + nd : 9 + nd, :]), base(prm_pair[pl.ds(8 + dest, 1), :])
        rows = slice(64 * nd, 64 * nd + 64)
        for n in range(4):
            source = block_of(n)
            own_hi, own_lo = split(jnp.where(shift == (nd - source).astype(F32), here, 0.0))
            step = (dest - source).astype(F32)
            pair_hi, pair_lo = split(jnp.where(shift == step + far, there, 0.0))
            halo_hi, halo_lo = split(jnp.where(shift == step - far, there * inside, 0.0))
            at = 128 * n
            below = slice(256 + 64 * nd, 320 + 64 * nd)
            ww[rows, at : at + 128] = own_hi
            ww[rows, 512 + at : 640 + at] = own_hi
            w_lo[rows, at : at + 128] = own_lo
            ww[below, at : at + 128] = pair_hi
            ww[below, 512 + at : 640 + at] = pair_hi
            w_lo[below, at : at + 128] = pair_lo
            wh[n, rows, 0:128] = halo_hi
            wh[n, rows, 128:256] = halo_hi
            wh_lo[n, rows, :] = halo_lo
    e_copy.wait()

    def spectrum(a, b, i, at, depth):
        re = jnp.concatenate([a[i, 0], b[i, 0]], axis=0)
        im = jnp.concatenate([a[i, 1], b[i, 1]], axis=0)
        for half_p, parts in enumerate(butterflies(re, im, tw)):
            for j, pieces in enumerate(parts):
                for half, w in enumerate(pieces):
                    hi, lo = split(w)
                    l_hi[half_p, 64 * j : 64 * j + 64, 256 * half : 256 * half + 256] = hi
                    l_lo[half_p, 64 * j : 64 * j + 64, 256 * half : 256 * half + 256] = lo
        even, uneven = (
            dot(l_hi[k], t_hi[k]) + dot(l_lo[k], t_hi[k]) + dot(l_hi[k], t_lo[k]) for k in range(2)
        )
        early = lax.broadcasted_iota(jnp.int32, (64, 128), 1) < 64
        for j in range(4):
            for b4 in range(4):
                first, second = (even, uneven) if b4 % 2 == 0 else (uneven, even)
                rows = slice(64 * j, 64 * j + 64)
                c0 = 128 * (b4 // 2)
                u = jnp.where(early, first[rows, c0 : c0 + 128], second[rows, c0 : c0 + 128])
                v = jnp.where(early, first[rows, 256 + c0 : 384 + c0], second[rows, 256 + c0 : 384 + c0])
                e0 = 512 * b4 + 128 * j
                c, w = (
                    jnp.concatenate([e_own[part, :, e0 : e0 + 128], e_other[part, :, e0 : e0 + 128]], axis=0)
                    for part in range(2)
                )
                for half, value in enumerate((u * c - v * w, u * w + v * c)):
                    hi, lo = split(value)
                    spec[b4, pl.ds(at + 64 * half, 64), 128 * j : 128 * j + 128] = hi
                    spec[b4, pl.ds(depth + at + 64 * half, 64), 128 * j : 128 * j + 128] = lo

    def block_at(dg, dh):
        return 2 * lax.rem(g + dg, 2) + lax.rem(h + dh, 2)

    def near_copy(ii):
        return remote(near.at[1, ii], near_in.at[ii], near_s.at[ii], near_r.at[ii], core)

    def dest_rows(n):
        return pl.ds(pl.multiple_of(64 * (3 - block_of(n)), 64), 64)

    def row_copy(dg, n):
        at = dest_rows(n)
        return remote(side.at[dg, 0, at], side_in.at[dg, 0, at], row_s.at[dg, n], row_r.at[dg, n], peer(dg, 0, 1))

    def all_copy(dg):
        return remote(side.at[dg, 1], side_in.at[dg, 1], all_s.at[dg], all_r.at[dg], peer(dg, 0, 1))

    def opp_cross(i):
        return remote(opp.at[i], relay_in.at[i], rel_s.at[i], rel_r.at[i], peer(0, 1, 1))

    def opp_direct(i):
        return remote(opp.at[i], relay_in.at[i], rel_s.at[i], rel_r.at[i], peer(0, 0, 1))

    def cross_copy(dg, i):
        return remote(cross.at[dg, i], cross_in.at[dg, i], crs_s.at[dg, i], crs_r.at[dg, i], peer(dg, 1, 1))

    for i in range(2, 8):
        snd_copy(i).wait_recv()

    def own_rows(ii):
        def one(n, carry):
            @pl.when(jnp.logical_and(ii == 0, n == 2))
            def _():
                a_copy(2).start()
                b_copy(2).start()

            spectrum(keep, other, 4 * ii + n, pl.multiple_of(128 * n, 128), 512)
            return carry

        lax.fori_loop(0, 4, one, 0)
        for dg in range(2):
            for dh in range(2):
                b4 = block_at(dg, dh)
                total = dot(ww[...], spec[b4]) + dot(w_lo[...], spec[b4, 0:512, :])
                if dh == 0:
                    near[dg, ii] = total[0:256]
                else:
                    side[dg, ii] = total[0:256]
                pp[2 * dg + dh, ii] = total[256:512]
        near_copy(ii).start()

    def collect(i):
        n, ii = lax.rem(i, 4), i // 4
        at = dest_rows(n)
        for dg in range(2):
            cross_copy(dg, i).wait()
        parts = [
            near[0, ii, at, :] + side_in[0, ii, at, :] + cross_in[0, i],
            near_in[ii, at, :] + side_in[1, ii, at, :] + cross_in[1, i],
        ]
        hi, lo = split(jnp.concatenate(parts, axis=0))
        order = perm[h]
        rows = dot(hi, order) + dot(lo, order)
        for dg in range(2):
            row = 4 * (3 - block_of(n)) + 2 * lax.rem(g + dg, 2) + ii
            for c in range(4):
                by_lane[c][pl.ds(row, 64, stride=16), :] = rows[64 * dg : 64 * dg + 64, 128 * c : 128 * c + 128]

    def step(i, carry):
        n, ii = lax.rem(i, 4), i // 4

        @pl.when(jnp.logical_or(i == 0, i == 3))
        def _():
            own_rows(i // 3)

            @pl.when(i == 3)
            def _():
                for dg in range(2):
                    all_copy(dg).start()

        a_copy(i).wait_recv()
        b_copy(i).wait_recv()

        @pl.when(i < 5)
        def _():
            a_copy(i).wait_send()
            b_copy(i).wait_send()
            a_copy(i + 3).start()
            b_copy(i + 3).start()

        spectrum(halo_a, halo_b, i, 0, 128)
        mine = pl.ds(pl.multiple_of(64 * n, 64), 64)
        for dh in range(2):
            for dg in range(2):
                b4 = block_at(dg, dh)
                total = dot(wh[n], spec[b4, 0:256, :]) + dot(wh_lo[n], spec[b4, 0:128, :])
                pp[2 * dg + dh, ii] = pp[2 * dg + dh, ii] + total
                if dh == 0:
                    opp[i, dg] = pp[2 * dg, ii, mine, :]
                else:
                    cross[dg, i] = pp[2 * dg + 1, ii, mine, :]
            if dh == 0:

                @pl.when(i < 4)
                def _():
                    opp_cross(i).start()

                @pl.when(i >= 4)
                def _():
                    opp_direct(i).start()

        @pl.when(i < 4)
        def _():
            for dg in range(2):
                cross_copy(dg, i).start()

        @pl.when(jnp.logical_and(i >= 1, i < 5))
        def _():
            opp_cross(i - 1).wait()
            at = dest_rows(i - 1)
            for dg in range(2):
                side[dg, 0, at, :] = side[dg, 0, at, :] + relay_in[i - 1, dg]
                row_copy(dg, i - 1).start()

        @pl.when(i >= 5)
        def _():
            forward(i - 1)

        @pl.when(i >= 4)
        def _():
            @pl.when(i == 4)
            def _():
                near_copy(0).wait()

            for dg in range(2):
                row_copy(dg, i - 4).wait()
            collect(i - 4)

        return carry

    def forward(i):
        opp_direct(i).wait()
        for dg in range(2):
            cross[dg, i] = cross[dg, i] + relay_in[i, dg]
            cross_copy(dg, i).start()

    lax.fori_loop(0, 8, step, 0)
    forward(7)
    near_copy(1).wait()
    for dg in range(2):
        all_copy(dg).wait()

    def last(i, carry):
        collect(i)
        return carry

    lax.fori_loop(4, 8, last, 0)
    results = [
        pltpu.make_async_copy(by_lane[c], out.at[:, pl.ds(128 * c, 128)], load_sem.at[c]) for c in range(4)
    ]
    for c in results:
        c.start()
    for i in range(8):
        snd_copy(i).wait_send()
        if i >= 5:
            a_copy(i).wait_send()
            b_copy(i).wait_send()
    for c in results:
        c.wait()


def local(strips, field, spectral_phase, chirp_shift, tile_map, tile_phase):
    waves, tw = dft_tables()
    vmem = pl.BlockSpec(memory_space=pltpu.VMEM)
    hbm = pl.BlockSpec(memory_space=pl.ANY)
    rows = pltpu.VMEM((8, 2, 32, 1024), F32)
    small = pltpu.VMEM((16, 128), F32)
    phase = pltpu.VMEM((2, 32, NY), F32)
    sums = pltpu.VMEM((2, 2, 256, 512), F32)
    dma = pltpu.SemaphoreType.DMA
    out = pl.pallas_call(
        functools.partial(kernel, strips),
        in_specs=[hbm, hbm, hbm, hbm, vmem, vmem, pl.BlockSpec(memory_space=pltpu.SMEM)],
        out_specs=hbm,
        out_shape=jax.ShapeDtypeStruct((1024, 512), F32),
        scratch_shapes=[
            pltpu.VMEM((8, 2, 512, 128), F32),
            rows, rows, rows, rows, rows,
            small, small, small, small,
            pltpu.VMEM((32, NY), F32),
            pltpu.VMEM(waves.shape, F32),
            pltpu.VMEM(tw.shape, F32),
            phase, phase,
            pltpu.VMEM((2, 512, 512), BF),
            pltpu.VMEM((2, 512, 512), BF),
            pltpu.VMEM((2, 512, 512), BF),
            pltpu.VMEM((512, 1024), BF),
            pltpu.VMEM((512, 512), BF),
            pltpu.VMEM((4, 256, 256), BF),
            pltpu.VMEM((4, 256, 128), BF),
            pltpu.VMEM((2, 256, 512), BF),
            pltpu.VMEM((2, 256, 512), BF),
            pltpu.VMEM((4, 1024, 512), BF),
            sums,
            pltpu.VMEM((2, 256, 512), F32),
            sums, sums,
            pltpu.VMEM((4, 2, 256, 512), F32),
            pltpu.VMEM((8, 2, 64, 512), F32),
            pltpu.VMEM((8, 2, 64, 512), F32),
            pltpu.VMEM((2, 8, 64, 512), F32),
            pltpu.VMEM((2, 8, 64, 512), F32),
            *[pltpu.VMEM((1024, 128), F32)] * 4,
            dma((11,)),
            *[dma((8,))] * 6,
            dma((3,)), dma((3,)),
            dma((2,)), dma((2,)),
            dma((2, 4)), dma((2, 4)),
            dma((2,)), dma((2,)),
            dma((8,)), dma((8,)),
            dma((2, 8)), dma((2, 8)),
        ],
        compiler_params=pltpu.CompilerParams(
            collective_id=0, has_side_effects=True, vmem_limit_bytes=60 * 2**20
        ),
        cost_estimate=pl.CostEstimate(flops=40 * 10**9, bytes_accessed=10 * 2**20, transcendentals=0),
    )(
        field.reshape(2, 512, 1024), spectral_phase, jnp.asarray(waves), jnp.asarray(tw),
        chirp_shift.reshape(1, 32), tile_phase, tile_map,
    )
    return out.reshape(2, NT, 16, 512)


def solution(mesh):
    placed = (P(None, "freq", "xs", "yh"), P("freq", None), P("freq"), P("xs"), P(None, "freq"))
    return jax.shard_map(
        functools.partial(local, mesh.shape["xs"]),
        mesh=mesh,
        in_specs=placed,
        out_specs=P(None, None, "xs", ("freq", "yh")),
        check_vma=False,
    )
```

profile of v0, /device:TPU:1, one launch (start us, length us, event | category | flops | bytes accessed | tf_op | source)
XLA Modules:
  0.0 130.4 jit_solution(6348255374160613960)
XLA Ops:
  0.0 127.2 %shard_map.73 = f32[1024,512]{1,0:T(8,128)} custom-call(f32[2,512,1024]{2,1,0:T(8,128)} %bitcast.4, f32[32,2048]{1,0:T(8,128)} %phi_hbm.1, f32[2,2,256,256]{3,2,1,0:T(8,128)} %constant.4.clone.waves_hbm, f32[2,8,256]{2,1,0:T(8,128)} %constant.5.clone.tw_hbm, s32[1,32]{1,0:T(1,128)} %bitcast.5, f32[4,32]{1,0:T(4,128)} %tile_phase.1, s32[4]{0:T(128)} %tile_ids.1), custom_call_target="tpu_custom_call" | custom-call | flops 40000000000 | bytes 10485760 | tf_op jit(solution)/shard_map/pallas_call | solution.py:453
  127.2 3.2 %copy.9 = f32[2,32,16,512]{3,2,1,0:T(8,128)} copy(f32[2,32,16,512]{3,2,1,0:T(8,128)} %bitcast.3) | data formatting | bytes 4194304
where the time goes:
time: 131 us; the launch traced here: 130 us
  Pallas kernels  127 us (97%)
  local copies, waits for them, and re-layouts  3.22 us (2%)
    pallas_call x1, Pallas kernels, local(): pl.pallas_call(functools.partial(kernel, strips), in_specs=[hbm, hbm, hbm...  127 us
    unnamed x1, local copies, waits for them, and re-layouts  3.22 us

commit v1 on v0

--- a/solution.py
+++ b/solution.py
@@ -12,6 +12,7 @@
 NF = 64
 NY = 2048
 NT = 32
+VMEM = 58
 BF = jnp.bfloat16
 F32 = jnp.float32
 AXES = ("freq", "xs", "yh")
@@ -39,6 +40,18 @@
 
 def dot_t(a, b):
     return lax.dot_general(a, b, (((1,), (1,)), ((), ())), preferred_element_type=F32)
+
+
+def sincos(x):
+    k = jnp.floor(x * (2.0 / math.pi) + 0.5)
+    r = ((x - k * 1.5703125) - k * 4.837512969970703125e-4) - k * 7.54978995489188216e-8
+    z = r * r
+    sine = r + r * z * (-1.6666654611e-1 + z * (8.3321608736e-3 - z * 1.9515295891e-4))
+    cosine = (1.0 - 0.5 * z) + z * z * (4.166664568298827e-2 + z * (-1.388731625493765e-3 + z * 2.443315711809948e-5))
+    half = jnp.floor(k * 0.5)
+    swap = (k - 2.0 * half) > 0.5
+    sign = 1.0 - 2.0 * (half - 2.0 * jnp.floor(half * 0.5))
+    return sign * jnp.where(swap, cosine, sine), sign * jnp.where(swap, -sine, cosine)
 
 
 def butterflies(re, im, tw):
@@ -81,17 +94,28 @@
     strips, field, phi_hbm, waves_hbm, tw_hbm, shift_row, tile_phase, tile_ids, out,
     flat, snd, keep, other, halo_a, halo_b, prm, prm_out, prm_in, prm_pair,
     phi, waves, tw, e_own, e_other, t_hi, t_lo, perm, ww, w_lo, wh, wh_lo,
-    l_hi, l_lo, spec, near, near_in, side, side_in, pp, opp, relay_in, cross, cross_in, *rest,
+    l_hi, l_lo, spec, near, near_in, side, side_in, pp, opp, relay_in, cross, cross_in, via_1, via_2, *rest,
 ):
     by_lane = rest[:4]
     (load_sem, snd_s, snd_r, ha_s, ha_r, hb_s, hb_r, prm_s, prm_r,
-     near_s, near_r, row_s, row_r, all_s, all_r, rel_s, rel_r, crs_s, crs_r) = rest[4:]
+     near_s, near_r, row_s, row_r, rel_s, rel_r, crs_s, crs_r, v1_s, v1_r, v2_s, v2_r) = rest[4:]
     g, s, h = (lax.axis_index(a) for a in AXES)
     odd = lax.rem(s, 2)
     pair = s + 1 - 2 * odd
     onward = lax.rem(s + strips + 4 * odd - 2, strips)
     back = lax.rem(s + strips + 2 - 4 * odd, strips)
     core = (1 - g, s, h)
+
+    z, y, turns = s // 8, lax.rem(s // 2, 4), strips // 8
+    hop = 1 - 2 * odd
+    across = 8 * z + 2 * lax.rem(y + 4 + hop, 4) + odd
+    across_from = 8 * z + 2 * lax.rem(y + 4 - hop, 4) + odd
+    z_on = 8 * lax.rem(z + turns - hop, turns) + odd
+    z_back = 8 * lax.rem(z + turns + hop, turns) + odd
+    leaves = (y == 2 - odd).astype(jnp.int32)
+    third = across + leaves * (z_on + 2 * (3 - 3 * odd) - across)
+    enters = (y == 3 - 3 * odd).astype(jnp.int32)
+    third_from = across_from + enters * (z_back + 2 * (2 - odd) - across_from)
 
     def peer(dg, ds, dh):
         return (lax.rem(g + dg, 2), pair if ds else s, lax.rem(h + dh, 2))
@@ -115,6 +139,7 @@
         c.start()
     barrier = pltpu.get_barrier_semaphore()
     greet = [core, peer(0, 0, 1), peer(1, 0, 1), peer(0, 1, 1), peer(1, 1, 1), (g, onward, h), (g, back, h)]
+    greet += [(g, across, h), (g, across_from, h), (g, third, h), (g, third_from, h)]
     for to in greet:
         pl.semaphore_signal(barrier, inc=1, device_id=to, device_id_type=MESH)
 
@@ -126,6 +151,23 @@
 
     def b_copy(i):
         return remote(other.at[i], halo_b.at[i], hb_s.at[i], hb_r.at[i], (g, onward, h))
+
+    def via_copy(hops, k, which):
+        i = 4 + 3 * k
+        if hops == 1:
+            src = (keep, other)[which].at[i]
+            return remote(src, via_1.at[k, which], v1_s.at[k, which], v1_r.at[k, which], (g, across, h))
+        if hops == 2:
+            return remote(
+                via_1.at[k, which], via_2.at[k, which], v2_s.at[k, which], v2_r.at[k, which], (g, across, h)
+            )
+        dst, sems = ((halo_a, (ha_s, ha_r)), (halo_b, (hb_s, hb_r)))[which]
+        return remote(via_2.at[k, which], dst.at[i], sems[0].at[i], sems[1].at[i], (g, third, h))
+
+    def pass_on(hops, k):
+        for which in range(2):
+            via_copy(hops - 1, k, which).wait_recv()
+            via_copy(hops, k, which).start()
 
     def gather_rows(i, whose, into):
         row = 4 * block_of(lax.rem(i, 4)) + 2 * whose + i // 4
@@ -146,10 +188,6 @@
     for c in loads:
         c.wait()
 
-    def pack_first(i, carry):
-        gather_rows(i, g, keep)
-        return carry
-
     def pack_send(i, carry):
         gather_rows(i, 1 - g, snd)
         snd_copy(i).start()
@@ -159,27 +197,34 @@
         gather_rows(i, g, keep)
         return carry
 
-    lax.fori_loop(0, 2, pack_first, 0)
+    for i in (0, 4, 1):
+        gather_rows(i, g, keep)
     pl.semaphore_wait(barrier, len(greet))
     a_copy(0).start()
+    via_copy(1, 0, 0).start()
     a_copy(1).start()
     lax.fori_loop(0, 8, pack_send, 0)
     prm_core.start()
     prm_strip.start()
-    lax.fori_loop(2, 8, pack_keep, 0)
-    for i in range(2):
+    lax.fori_loop(2, 4, pack_keep, 0)
+    lax.fori_loop(5, 8, pack_keep, 0)
+    for i in (0, 4, 1):
         snd_copy(i).wait_recv()
-        b_copy(i).start()
+        if i == 4:
+            via_copy(1, 0, 1).start()
+        else:
+            b_copy(i).start()
 
     for c in tables:
         c.wait()
-    lane = lax.broadcasted_iota(jnp.int32, (512, 512), 0)
-    wave = lax.broadcasted_iota(jnp.int32, (512, 512), 1)
+    lane = lax.broadcasted_iota(jnp.int32, (512, 1), 0)
+    wave = lax.broadcasted_iota(jnp.int32, (1, 512), 1)
     turn = lax.rem(lane, 128)
     for half in range(2):
         late = (turn >= 64).astype(jnp.int32)
         late = late if half == 0 else 1 - late
-        perm[half] = (8 * lax.rem(turn, 64) + 2 * (lane // 128) + late == wave).astype(F32).astype(BF)
+        target = 8 * lax.rem(turn, 64) + 2 * (lane // 128) + late
+        perm[half] = jnp.where(target == wave, 1.0, 0.0).astype(BF)
         c_hi, c_lo = split(waves[half, 0])
         s_hi, s_lo = split(waves[half, 1])
         for table, c, w in ((t_hi, c_hi, s_hi), (t_lo, c_lo, s_lo)):
@@ -189,13 +234,18 @@
             table[half, 256:512, 256:512] = c
 
     lanes = lax.rem(lax.broadcasted_iota(jnp.int32, (1, 512), 1), 128)
-    for b in range(4):
-        x = phi[:, 512 * b : 512 * b + 512]
-        late = lanes >= 64 if b % 2 == 0 else lanes < 64
+    for half in range(2):
+        late = lanes >= 64 if half == 0 else lanes < 64
         sign = 1.0 - 2.0 * jnp.where(late, h, 0).astype(F32)
-        for part, value in enumerate((jnp.cos(x), jnp.sin(x))):
-            hi, lo = split(value)
-            e_own[part, :, 512 * b : 512 * b + 512] = (dot_t(hi, perm[b % 2]) + dot_t(lo, perm[b % 2])) * sign
+        stack = []
+        for b in (half, half + 2):
+            sine, cosine = sincos(phi[:, 512 * b : 512 * b + 512])
+            stack += [*split(cosine), *split(sine)]
+        got = dot_t(jnp.concatenate(stack, axis=0), perm[half])
+        for k, b in enumerate((half, half + 2)):
+            for part in range(2):
+                at = 128 * k + 64 * part
+                e_own[part, :, 512 * b : 512 * b + 512] = (got[at : at + 32] + got[at + 32 : at + 64]) * sign
     e_copy = remote(e_own, e_other, prm_s.at[2], prm_r.at[2], core)
     e_copy.start()
 
@@ -213,7 +263,8 @@
         phase = jnp.zeros((1, 128), F32)
         for t in range(4):
             phase = phase + jnp.where(tile == float(t), both[1 + t : 2 + t, :], 0.0)
-        re, im = jnp.cos(angle + phase) * scale, jnp.sin(angle + phase) * scale
+        im, re = sincos(angle + phase)
+        im, re = im * scale, re * scale
         return jnp.concatenate([jnp.where(real_in, re, -im), jnp.where(real_in, im, re)], axis=0)
 
     far = (4 * (1 - 2 * odd)).astype(F32)
@@ -239,6 +290,11 @@
             wh[n, rows, 0:128] = halo_hi
             wh[n, rows, 128:256] = halo_hi
             wh_lo[n, rows, :] = halo_lo
+    for i in (2, 3, 5, 6, 7):
+        snd_copy(i).wait_recv()
+    pass_on(2, 0)
+    for which in range(2):
+        via_copy(1, 1, which).start()
     e_copy.wait()
 
     def spectrum(a, b, i, at, depth):
@@ -280,12 +336,9 @@
     def dest_rows(n):
         return pl.ds(pl.multiple_of(64 * (3 - block_of(n)), 64), 64)
 
-    def row_copy(dg, n):
-        at = dest_rows(n)
-        return remote(side.at[dg, 0, at], side_in.at[dg, 0, at], row_s.at[dg, n], row_r.at[dg, n], peer(dg, 0, 1))
-
-    def all_copy(dg):
-        return remote(side.at[dg, 1], side_in.at[dg, 1], all_s.at[dg], all_r.at[dg], peer(dg, 0, 1))
+    def row_copy(dg, i):
+        at, ii = dest_rows(lax.rem(i, 4)), i // 4
+        return remote(side.at[dg, ii, at], side_in.at[dg, ii, at], row_s.at[dg, i], row_r.at[dg, i], peer(dg, 0, 1))
 
     def opp_cross(i):
         return remote(opp.at[i], relay_in.at[i], rel_s.at[i], rel_r.at[i], peer(0, 1, 1))
@@ -295,9 +348,6 @@
 
     def cross_copy(dg, i):
         return remote(cross.at[dg, i], cross_in.at[dg, i], crs_s.at[dg, i], crs_r.at[dg, i], peer(dg, 1, 1))
-
-    for i in range(2, 8):
-        snd_copy(i).wait_recv()
 
     def own_rows(ii):
         def one(n, carry):
@@ -319,6 +369,9 @@
                 else:
                     side[dg, ii] = total[0:256]
                 pp[2 * dg + dh, ii] = total[256:512]
+        for n in (1, 3):
+            for dg in range(2):
+                row_copy(dg, 4 * ii + n).start()
         near_copy(ii).start()
 
     def collect(i):
@@ -330,35 +383,59 @@
             near[0, ii, at, :] + side_in[0, ii, at, :] + cross_in[0, i],
             near_in[ii, at, :] + side_in[1, ii, at, :] + cross_in[1, i],
         ]
-        hi, lo = split(jnp.concatenate(parts, axis=0))
-        order = perm[h]
-        rows = dot(hi, order) + dot(lo, order)
+        got = dot(jnp.concatenate(split(jnp.concatenate(parts, axis=0)), axis=0), perm[h])
+        rows = got[0:128] + got[128:256]
         for dg in range(2):
             row = 4 * (3 - block_of(n)) + 2 * lax.rem(g + dg, 2) + ii
             for c in range(4):
                 by_lane[c][pl.ds(row, 64, stride=16), :] = rows[64 * dg : 64 * dg + 64, 128 * c : 128 * c + 128]
 
+    def relay(i):
+        n, ii = lax.rem(i, 4), i // 4
+
+        @pl.when(lax.rem(i, 2) == 0)
+        def _():
+            opp_cross(i).wait()
+            at = dest_rows(n)
+            for dg in range(2):
+                side[dg, ii, at, :] = side[dg, ii, at, :] + relay_in[i, dg]
+                row_copy(dg, i).start()
+
+        @pl.when(lax.rem(i, 2) == 1)
+        def _():
+            opp_direct(i).wait()
+            for dg in range(2):
+                cross[dg, i] = cross[dg, i] + relay_in[i, dg]
+                cross_copy(dg, i).start()
+
     def step(i, carry):
         n, ii = lax.rem(i, 4), i // 4
 
+        @pl.when(i == 2)
+        def _():
+            pass_on(3, 0)
+
+        @pl.when(i == 3)
+        def _():
+            pass_on(2, 1)
+
+        @pl.when(i == 5)
+        def _():
+            pass_on(3, 1)
+
         @pl.when(jnp.logical_or(i == 0, i == 3))
         def _():
             own_rows(i // 3)
-
-            @pl.when(i == 3)
-            def _():
-                for dg in range(2):
-                    all_copy(dg).start()
 
         a_copy(i).wait_recv()
         b_copy(i).wait_recv()
 
-        @pl.when(i < 5)
-        def _():
-            a_copy(i).wait_send()
-            b_copy(i).wait_send()
-            a_copy(i + 3).start()
-            b_copy(i + 3).start()
+        for now, start in ((0, 3), (2, 5), (3, 6)):
+
+            @pl.when(i == now)
+            def _():
+                a_copy(start).start()
+                b_copy(start).start()
 
         spectrum(halo_a, halo_b, i, 0, 128)
         mine = pl.ds(pl.multiple_of(64 * n, 64), 64)
@@ -373,30 +450,22 @@
                     cross[dg, i] = pp[2 * dg + 1, ii, mine, :]
             if dh == 0:
 
-                @pl.when(i < 4)
+                @pl.when(lax.rem(i, 2) == 0)
                 def _():
                     opp_cross(i).start()
 
-                @pl.when(i >= 4)
+                @pl.when(lax.rem(i, 2) == 1)
                 def _():
                     opp_direct(i).start()
 
-        @pl.when(i < 4)
+        @pl.when(lax.rem(i, 2) == 0)
         def _():
             for dg in range(2):
                 cross_copy(dg, i).start()
 
-        @pl.when(jnp.logical_and(i >= 1, i < 5))
-        def _():
-            opp_cross(i - 1).wait()
-            at = dest_rows(i - 1)
-            for dg in range(2):
-                side[dg, 0, at, :] = side[dg, 0, at, :] + relay_in[i - 1, dg]
-                row_copy(dg, i - 1).start()
-
-        @pl.when(i >= 5)
-        def _():
-            forward(i - 1)
+        @pl.when(i >= 1)
+        def _():
+            relay(i - 1)
 
         @pl.when(i >= 4)
         def _():
@@ -410,19 +479,13 @@
 
         return carry
 
-    def forward(i):
-        opp_direct(i).wait()
+    lax.fori_loop(0, 8, step, 0)
+    relay(7)
+    near_copy(1).wait()
+
+    def last(i, carry):
         for dg in range(2):
-            cross[dg, i] = cross[dg, i] + relay_in[i, dg]
-            cross_copy(dg, i).start()
-
-    lax.fori_loop(0, 8, step, 0)
-    forward(7)
-    near_copy(1).wait()
-    for dg in range(2):
-        all_copy(dg).wait()
-
-    def last(i, carry):
+            row_copy(dg, i).wait()
         collect(i)
         return carry
 
@@ -434,9 +497,13 @@
         c.start()
     for i in range(8):
         snd_copy(i).wait_send()
-        if i >= 5:
+        if i not in (4, 7):
             a_copy(i).wait_send()
             b_copy(i).wait_send()
+    for hops in range(1, 4):
+        for k in range(2):
+            for which in range(2):
+                via_copy(hops, k, which).wait_send()
     for c in results:
         c.wait()
 
@@ -444,7 +511,7 @@
 def local(strips, field, spectral_phase, chirp_shift, tile_map, tile_phase):
     waves, tw = dft_tables()
     vmem = pl.BlockSpec(memory_space=pltpu.VMEM)
-    hbm = pl.BlockSpec(memory_space=pl.ANY)
+    hbm = pl.BlockSpec(memory_space=pltpu.HBM)
     rows = pltpu.VMEM((8, 2, 32, 1024), F32)
     small = pltpu.VMEM((16, 128), F32)
     phase = pltpu.VMEM((2, 32, NY), F32)
@@ -453,7 +520,7 @@
     out = pl.pallas_call(
         functools.partial(kernel, strips),
         in_specs=[hbm, hbm, hbm, hbm, vmem, vmem, pl.BlockSpec(memory_space=pltpu.SMEM)],
-        out_specs=hbm,
+        out_specs=pl.BlockSpec(memory_space=pl.ANY),
         out_shape=jax.ShapeDtypeStruct((1024, 512), F32),
         scratch_shapes=[
             pltpu.VMEM((8, 2, 512, 128), F32),
@@ -481,18 +548,20 @@
             pltpu.VMEM((8, 2, 64, 512), F32),
             pltpu.VMEM((2, 8, 64, 512), F32),
             pltpu.VMEM((2, 8, 64, 512), F32),
+            pltpu.VMEM((2, 2, 2, 32, 1024), F32),
+            pltpu.VMEM((2, 2, 2, 32, 1024), F32),
             *[pltpu.VMEM((1024, 128), F32)] * 4,
             dma((11,)),
             *[dma((8,))] * 6,
             dma((3,)), dma((3,)),
             dma((2,)), dma((2,)),
-            dma((2, 4)), dma((2, 4)),
-            dma((2,)), dma((2,)),
+            dma((2, 8)), dma((2, 8)),
             dma((8,)), dma((8,)),
             dma((2, 8)), dma((2, 8)),
+            *[dma((2, 2))] * 4,
         ],
         compiler_params=pltpu.CompilerParams(
-            collective_id=0, has_side_effects=True, vmem_limit_bytes=60 * 2**20
+            collective_id=0, has_side_effects=True, vmem_limit_bytes=VMEM * 2**20
         ),
         cost_estimate=pl.CostEstimate(flops=40 * 10**9, bytes_accessed=10 * 2**20, transcendentals=0),
     )(

time: 131 us -> 117 us (0.89)
  Pallas kernels: 127 us -> 113 us
    pallas_call x1, Pallas kernels: 127 us -> 113 us  [local(): pl.pallas_call(functools.partial(kernel, strips), in_specs=[hbm, hbm, hbm...]
where the time goes in v1:
time: 117 us; the launch traced here: 116 us
  Pallas kernels  113 us (97%)
  local copies, waits for them, and re-layouts  3.22 us (3%)
    pallas_call x1, Pallas kernels, local(): pl.pallas_call(functools.partial(kernel, strips), in_specs=[hbm, hbm, hbm...  113 us
    unnamed x1, local copies, waits for them, and re-layouts  3.22 us

profile of v1, /device:TPU:1, one launch (start us, length us, event | category | flops | bytes accessed | tf_op | source)
XLA Modules:
  0.0 116.1 jit_solution(14036757936496191549)
XLA Ops:
  0.0 112.9 %shard_map.73 = f32[1024,512]{1,0:T(8,128)} custom-call(f32[2,512,1024]{2,1,0:T(8,128)} %bitcast.4, f32[32,2048]{1,0:T(8,128)} %phi_hbm.1, f32[2,2,256,256]{3,2,1,0:T(8,128)} %constant.4.clone.waves_hbm, f32[2,8,256]{2,1,0:T(8,128)} %constant.5.clone.tw_hbm, s32[1,32]{1,0:T(1,128)} %bitcast.5, f32[4,32]{1,0:T(4,128)} %tile_phase.1, s32[4]{0:T(128)} %tile_ids.1), custom_call_target="tpu_custom_call" | custom-call | flops 40000000000 | bytes 10485760 | tf_op jit(solution)/shard_map/pallas_call | solution.py:520
  112.9 3.2 %copy.9 = f32[2,32,16,512]{3,2,1,0:T(8,128)} copy(f32[2,32,16,512]{3,2,1,0:T(8,128)} %bitcast.3) | data formatting | bytes 4194304
